TPU v7x, 512 devices: a whole 4x8x8 slice. The times are simulated.
512 devices in a mesh: row: 32 (over z, y_hi), col: 16 (over y_lo, x, core).
Axes of the slice: x: 4, y: 8 (y_hi: 4, y_lo: 2; y = y_hi * 2 + y_lo), z: 8, core: 2. Of those that a mesh axis runs over, the one named last changes fastest.
Arguments:
- orbitals: bfloat16 [20480, 384], P(('row', 'col')), may hold values from -6 to 6
- coulomb: float32 [20480, 20480], P('row', 'col'), may hold values from -0.001953125 to 0.001953125
- interp: bfloat16 [16384, 20480], P('row', 'col'), may hold values from -0.0390625 to 0.0390625
Outputs:
- exchanged: bfloat16 [16384, 384], P(('row', 'col'))
All inputs are finite; a program needn't handle non-finite values.
Results may differ from a plain program's by a relative error of at most 0.018.
Values may be sent and summed in bfloat16 or wider, within the bound.
A program may use at most 64 MiB of HBM per device.

v0:
```python
import jax
import jax.numpy as jnp
from jax import lax
from jax.sharding import PartitionSpec as P


def broadcast(value, axis, source):
    kept = jnp.where(lax.axis_index(axis) == source, value, 0).astype(value.dtype)
    return lax.psum(kept, axis)


def local(orbitals, coulomb, interp):
    near = lax.all_gather(orbitals, "col", axis=0, tiled=True)
    factor = lax.axis_size("row") // lax.axis_size("col")
    column = lax.axis_index("col")
    pieces = []
    for offset in range(factor):
        pieces.append(broadcast(near, "row", column * factor + offset))
    far = jnp.concatenate(pieces, 0)
    density = lax.dot_general(
        near, far, (((1,), (1,)), ((), ())), preferred_element_type=jnp.float32
    )
    weighted = (coulomb * density).astype(jnp.bfloat16)
    partial_sum = lax.dot_general(
        weighted, near, (((0,), (0,)), ((), ())), preferred_element_type=jnp.float32
    )
    summed = lax.psum(partial_sum, "row")
    contracted = summed.astype(jnp.bfloat16)
    terms = jnp.dot(interp, contracted, preferred_element_type=jnp.float32)
    return lax.psum_scatter(terms.astype(jnp.bfloat16), "col", scatter_dimension=0, tiled=True)


def solution(mesh):
    in_specs = (P(("row", "col"), None), P("row", "col"), P("row", "col"))
    out_specs = P(("row", "col"), None)
    return jax.shard_map(local, mesh=mesh, in_specs=in_specs, out_specs=out_specs, check_vma=False)
```

profile of v0, /device:TPU:1, one launch (start us, length us, event | category | flops | bytes accessed | tf_op | source)
XLA Modules:
  0.0 610.5 jit_solution(2543077804153859087)
XLA Ops:
  6.5 0.0 copy-start
  6.5 0.0 all-reduce.4.cloned.1.call-start
  6.5 24.5 %all_gather.3 = bf16[640,384]{1,0:T(8,128)(2,1)S(1)} all-gather(bf16[40,384]{1,0:T(8,128)(2,1)} %param.3), channel_id=1, replica_groups=mesh['row'=32,'col'=16] {'col'}, dimensions={0}, use_global_device_ids=true | all-gather | bytes 522240 | tf_op jit(solution)/shard_map/all_gather | solution.py:13
  31.0 0.0 copy-start.1
  31.0 0.8 copy-done.1
  31.8 1.0 broadcast_select_fusion.1
  32.8 0.0 all-reduce.4.cloned.1.call-update
  32.9 0.0 reduce-scatter.4.cloned.1.call-start
  32.9 295.7 %all-reduce.4.cloned.1.call-done = (bf16[640,384]{1,0:T(8,128)(2,1)}, bf16[640,384]{1,0:T(8,128)(2,1)}) async-done(((bf16[640,384]{1,0:T(8,128)(2,1)}, bf16[640,384]{1,0:T(8,128)(2,1)}), (bf16[640,384]{1,0:T(8,128)(2,1)}, bf16[640,384]{1,0:T(8,128)(2,1)})) %all-reduce.4.cloned.1.call-update) | async-done | bytes 983056 | tf_op jit(solution)/shard_map/psum | solution.py:9
  328.6 4.4 fusion.2
  333.0 164.5 %all-reduce.5 = bf16[1280,384]{1,0:T(8,128)(2,1)} all-reduce(f32[1280,384]{1,0:T(8,128)S(1)} %fusion.2), channel_id=1, replica_groups=mesh['row'=32,'col'=16] {'row'}, use_global_device_ids=true, to_apply=%region_2.3 | all-reduce | flops 491520 | bytes 2949120 | tf_op jit(solution)/shard_map/psum | solution.py:27
  497.5 0.0 copy-done
  497.5 1.9 fusion.3
  499.5 0.9 copy.6
  500.4 0.0 reduce-scatter.4.cloned.1.call-update
  500.4 103.3 %reduce-scatter.4.cloned.1.call-done = bf16[32,384]{1,0:T(8,128)(2,1)} async-done(((bf16[512,384]{1,0:T(8,128)(2,1)}), bf16[32,384]{1,0:T(8,128)(2,1)}) %reduce-scatter.4.cloned.1.call-update) | async-done | bytes 24592 | tf_op jit(solution)/shard_map/reduce_scatter | solution.py:30
Async XLA Ops:
  6.5 491.0 %copy-start = (bf16[512,1280]{1,0:T(8,128)(2,1)S(1)}, bf16[512,1280]{1,0:T(8,128)(2,1)}, u32[]{:S(2)}) copy-start(bf16[512,1280]{1,0:T(8,128)(2,1)} %param.5) | copy-start | bytes 3932164
  6.5 322.0 %all-reduce.4.cloned.1.call-start = ((), (), s32[]{:S(2)}) async-start(), calls=%async_computation.2 | async-start | bytes 1966080 | tf_op jit(solution)/shard_map/psum | solution.py:9
  31.0 0.8 copy-start.1
  32.9 570.8 %reduce-scatter.4.cloned.1.call-start = ((), (), s32[]{:S(2)}) async-start(), calls=%async_computation.1 | async-start | bytes 417792 | tf_op jit(solution)/shard_map/reduce_scatter | solution.py:30
Sparse Core Ops, SparseCore 0:
  33.0 295.5 all-reduce.3
  500.5 103.1 reduce-scatter.3
where the time goes:
time: 612 us; the launch traced here: 611 us
  waiting for transfers between devices  399 us (65%)
  blocking collectives  189 us (31%)
  between operations  13.4 us (2%)
  matrix products  6.34 us (1%)
    psum x1, waiting for transfers between devices, broadcast(): return lax.psum(kept, axis)  296 us
    psum x1, blocking collectives, local(): summed = lax.psum(partial_sum, 'row')  165 us
    reduce_scatter x1, waiting for transfers between devices, local(): lax.psum_scatter(terms.astype(jnp.bfloat16), 'col', scatter_dimension=0,...  103 us
    all_gather x1, blocking collectives, local(): near = lax.all_gather(orbitals, 'col', axis=0, tiled=True)  24.5 us
  transfers between devices with their start and end apart: 2, of which 2 were waited for; matrix products, arithmetic and copies ran while one was open for 0% of the time, Pallas kernels for 0%

commit v1 on v0

v1 whole, which is shorter than its diff:
```python
import jax
import jax.numpy as jnp
from jax import lax
from jax.experimental import pallas as pl
from jax.experimental.pallas import tpu as pltpu
from jax.sharding import PartitionSpec as P

MESH = pl.DeviceIdType.MESH
Z, Y, L, X, C = 8, 4, 2, 4, 2
F32, BF16 = jnp.float32, jnp.bfloat16


def device(z, y, l, x, core):
    return (z * Y + y, (l * X + x) * C + core)


def rows(slots):
    n, h, k = slots.shape
    return slots.astype(F32).reshape(n * h, k)


def kernel(
    orb, coul_hbm, interp_hbm, out,
    coul, coul_t, interp, near_s, near, far, acc_in, acc_out, part,
    y_out, y_in, con, con_m, terms, pair_out, pair_in, fin_out, fin_in,
    local_sem, near_ss, near_rs, sib_ss, sib_rs, perm_ss, perm_rs,
    far_ss, far_rs, acc_ss, acc_rs, ys_ss, ys_rs, yg_ss, yg_rs,
    con_ss, con_rs, pair_sem, fin_ss, fin_rs,
):
    row, col = lax.axis_index("row"), lax.axis_index("col")
    z, y = row // Y, row % Y
    l, x, core = col // (X * C), (col // C) % X, col % C
    up, down = device((z + 1) % Z, y, l, x, core), device((z + Z - 1) % Z, y, l, x, core)
    sibling = device(z, y, l, x, 1 - core)
    chips = [None] + [((l + k // X) % L, (x + k % X) % X) for k in range(1, L * X)]
    came = [None] + [((l + k // X) % L, (x + X - k % X) % X) for k in range(1, L * X)]
    ahead = [None] + [(y + k) % Y for k in range(1, Y)]
    behind = [None] + [(y + Y - k) % Y for k in range(1, Y)]
    sends = []

    def send(src, dst, ss, rs, to):
        copy = pltpu.make_async_remote_copy(
            src_ref=src, dst_ref=dst, send_sem=ss, recv_sem=rs, device_id=to, device_id_type=MESH
        )
        copy.start()
        sends.append(copy)
        return copy

    load_coul = pltpu.make_async_copy(coul_hbm, coul, local_sem.at[0])
    load_interp = pltpu.make_async_copy(interp_hbm, interp, local_sem.at[1])
    load_coul.start()
    load_interp.start()

    piece = (row % 2) * (L * X * C) + col
    target_col, target_z = row // 2, piece // Y
    targets = [(target_z * Y + j, target_col) for j in range(Y)]
    target_self = [(t[0] == row) & (t[1] == col) for t in targets]
    sources = []
    for j in range(Y):
        p = z * Y + j
        sources.append((2 * col + p // (L * X * C), p % (L * X * C)))
    source_self = [(s[0] == row) & (s[1] == col) for s in sources]

    barrier = pltpu.get_barrier_semaphore()
    greet = [up, down, sibling]
    greet += [device(z, y, chips[k][0], chips[k][1], core) for k in range(1, L * X)]
    greet += [device(z, ahead[k], l, x, core) for k in range(1, Y)]
    for d in greet:
        pl.semaphore_signal(barrier, inc=1, device_id=d, device_id_type=MESH)
    for j in range(Y):
        @pl.when(jnp.logical_not(source_self[j]))
        def _(j=j):
            pl.semaphore_signal(barrier, inc=1, device_id=sources[j], device_id_type=MESH)
    own_target = (target_col == col) & (target_z == z)
    pl.semaphore_wait(barrier, jnp.where(own_target, len(greet) + Y - 1, len(greet) + Y))

    kind = piece % Y

    def perm(j):
        return pltpu.make_async_remote_copy(
            src_ref=orb, dst_ref=far.at[piece], send_sem=perm_ss.at[j], recv_sem=perm_rs.at[kind],
            device_id=targets[j], device_id_type=MESH,
        )

    for j in range(Y):
        @pl.when(jnp.logical_not(target_self[j]))
        def _(j=j):
            perm(j).start()

        @pl.when(target_self[j])
        def _():
            far[piece] = orb[...]

    near_s[col] = orb[...]
    sib = [send(orb, near_s.at[col], sib_ss.at[0], sib_rs.at[0], sibling)]
    near_c = [None]
    for k in range(1, L * X):
        near_c.append(send(orb, near_s.at[col], near_ss.at[k], near_rs.at[k], device(z, y, *chips[k], core)))

    load_coul.wait()
    for k in range(coul.shape[1] // 128):
        coul_t[pl.ds(128 * k, 128), :] = coul[:, pl.ds(128 * k, 128)].T

    for k in range(1, L * X):
        near_c[k].wait_recv()
        slot = (came[k][0] * X + came[k][1]) * C + core
        sib.append(send(near_s.at[slot], near_s.at[slot], sib_ss.at[k], sib_rs.at[k], sibling))

    for j in range(Y):
        @pl.when(jnp.logical_not(source_self[j]))
        def _(j=j):
            pltpu.make_async_remote_copy(
                src_ref=orb, dst_ref=far.at[z * Y + j], send_sem=perm_ss.at[j], recv_sem=perm_rs.at[j],
                device_id=sources[j], device_id_type=MESH,
            ).wait_recv()

    def far_send(way, step, first, count):
        at = pl.ds(first, count)
        return send(far.at[at], far.at[at], far_ss.at[way, step], far_rs.at[way, step], (up, down)[way])

    far_c = [[far_send(0, 0, z * Y, Y)], [far_send(1, 0, z * Y, Y)]]
    for c in sib:
        c.wait_recv()
    near[...] = rows(near_s[...]).astype(BF16)

    def partial(block):
        points = rows(far[pl.ds(block * Y, Y)]).astype(BF16)
        density = lax.dot_general(points, near[...], (((1,), (1,)), ((), ())), preferred_element_type=F32)
        n = points.shape[0]
        weighted = (coul_t[pl.ds(pl.multiple_of(block * n, n), n), :] * density).astype(BF16)
        return jnp.dot(weighted, near[...], preferred_element_type=F32).reshape(Y, n // Y, -1)

    half = Y // 2
    own = partial(z)
    acc_out[0, 0, :half] = own[:half].astype(BF16)
    acc_out[1, 0, half:] = own[half:].astype(BF16)
    acc_c = [[], []]
    for way in range(2):
        at = pl.ds(half * way, half)
        acc_c[way].append(send(
            acc_out.at[way, 0, at], acc_in.at[way, 0, at],
            acc_ss.at[way, 0], acc_rs.at[way, 0], (up, down)[way]))
    for step in range(1, 4):
        blocks = ((z + Z - step) % Z, (z + step) % Z)
        for way in range(2):
            far_c[way][step - 1].wait_recv()
            if step < 3:
                far_c[way].append(far_send(way, step, blocks[way] * Y, Y))
            else:
                far_c[way].append(far_send(way, step, blocks[way] * Y + half * way, half))
        for way in range(2):
            share = partial(blocks[way])
            acc_c[way][step - 1].wait_recv()
            if step == 1:
                lo, hi = half * way, half * (way + 1)
                rest = slice(half, Y) if way == 0 else slice(0, half)
                acc_out[way, step, lo:hi] = (share[lo:hi] + acc_in[way, 0, lo:hi].astype(F32)).astype(BF16)
                acc_out[way, step, rest] = share[rest].astype(BF16)
            else:
                acc_out[way, step] = (share + acc_in[way, step - 1].astype(F32)).astype(BF16)
            acc_c[way].append(send(
                acc_out.at[way, step], acc_in.at[way, step],
                acc_ss.at[way, step], acc_rs.at[way, step], (up, down)[way]))
    far_c[0][3].wait_recv()
    far_c[1][3].wait_recv()
    block = (z + Z // 2) % Z
    share = partial(block)
    acc_c[0][3].wait_recv()
    acc_c[1][3].wait_recv()
    share = share + acc_in[0, 3].astype(F32) + acc_in[1, 3].astype(F32)
    part[...] = share
    y_out[...] = share.astype(BF16)

    ys = [None]
    for k in range(1, Y):
        ys.append(send(y_out.at[ahead[k]], y_in.at[k], ys_ss.at[k], ys_rs.at[k], device(z, ahead[k], l, x, core)))
    total = part[y]
    for k in range(1, Y):
        ys[k].wait_recv()
        total = total + y_in[k].astype(F32)
    mine = block * Y + y
    con[mine] = total.astype(BF16)
    yg = [None]
    for k in range(1, Y):
        yg.append(send(con.at[mine], con.at[mine], yg_ss.at[k], yg_rs.at[k], device(z, ahead[k], l, x, core)))
    for k in range(1, Y):
        yg[k].wait_recv()

    def con_send(way, step, first, count):
        at = pl.ds(first, count)
        return send(con.at[at], con.at[at], con_ss.at[way, step], con_rs.at[way, step], (up, down)[way])

    con_c = [[con_send(0, 0, block * Y, Y)], [con_send(1, 0, block * Y, Y)]]
    for step in range(1, 4):
        blocks = ((block + Z - step) % Z, (block + step) % Z)
        for way in range(2):
            con_c[way][step - 1].wait_recv()
            if step < 3:
                con_c[way].append(con_send(way, step, blocks[way] * Y, Y))
            else:
                con_c[way].append(con_send(way, step, blocks[way] * Y + half * way, half))
    load_interp.wait()
    con_c[0][3].wait_recv()
    con_c[1][3].wait_recv()
    con_m[...] = rows(con[...]).astype(BF16)
    terms[...] = jnp.dot(interp[...], con_m[...], preferred_element_type=F32).reshape(terms.shape)

    pair_out[...] = terms[:, 1 - core].astype(BF16)
    pair = send(pair_out, pair_in, pair_sem.at[0], pair_sem.at[1], sibling)
    pair.wait_recv()
    both = terms[:, core] + pair_in[...].astype(F32)
    terms[:, core] = both
    fin_out[...] = both.astype(BF16)
    fin = [None]
    for k in range(1, L * X):
        fin.append(send(
            fin_out.at[chips[k][0] * X + chips[k][1]], fin_in.at[k],
            fin_ss.at[k], fin_rs.at[k], device(z, y, *chips[k], core)))
    total = terms[l * X + x, core]
    for k in range(1, L * X):
        fin[k].wait_recv()
        total = total + fin_in[k].astype(F32)
    out[...] = total.astype(BF16)

    for c in sends:
        c.wait_send()
    for j in range(Y):
        @pl.when(jnp.logical_not(target_self[j]))
        def _(j=j):
            perm(j).wait_send()


def local(orbitals, coulomb, interp):
    h, k = orbitals.shape
    m, n = coulomb.shape
    g = interp.shape[0]
    out = g // (L * X * C)
    dma = pltpu.SemaphoreType.DMA
    return pl.pallas_call(
        kernel,
        out_shape=jax.ShapeDtypeStruct((out, k), BF16),
        in_specs=[
            pl.BlockSpec(memory_space=pltpu.VMEM),
            pl.BlockSpec(memory_space=pl.ANY),
            pl.BlockSpec(memory_space=pl.ANY),
        ],
        out_specs=pl.BlockSpec(memory_space=pltpu.VMEM),
        scratch_shapes=[
            pltpu.VMEM((m, n), F32),
            pltpu.VMEM((n, m), F32),
            pltpu.VMEM((g, n), BF16),
            pltpu.VMEM((L * X * C, h, k), BF16),
            pltpu.VMEM((m, k), BF16),
            pltpu.VMEM((Z * Y, h, k), BF16),
            pltpu.VMEM((2, 4, Y, h, k), BF16),
            pltpu.VMEM((2, 4, Y, h, k), BF16),
            pltpu.VMEM((Y, h, k), F32),
            pltpu.VMEM((Y, h, k), BF16),
            pltpu.VMEM((Y, h, k), BF16),
            pltpu.VMEM((Z * Y, h, k), BF16),
            pltpu.VMEM((n, k), BF16),
            pltpu.VMEM((L * X, C, out, k), F32),
            pltpu.VMEM((L * X, out, k), BF16),
            pltpu.VMEM((L * X, out, k), BF16),
            pltpu.VMEM((L * X, out, k), BF16),
            pltpu.VMEM((L * X, out, k), BF16),
            dma((2,)), dma((8,)), dma((8,)), dma((8,)), dma((8,)), dma((4,)), dma((4,)),
            dma((2, 4)), dma((2, 4)), dma((2, 4)), dma((2, 4)), dma((4,)), dma((4,)), dma((4,)), dma((4,)),
            dma((2, 4)), dma((2, 4)), dma((2,)), dma((8,)), dma((8,)),
        ],
        compiler_params=pltpu.CompilerParams(
            collective_id=0, has_side_effects=True, vmem_limit_bytes=40 * 1024 * 1024
        ),
        cost_estimate=pl.CostEstimate(
            flops=4 * m * n * k + 2 * g * n * k, bytes_accessed=4 * m * n + 2 * g * n, transcendentals=0
        ),
    )(orbitals, coulomb, interp)


def solution(mesh):
    in_specs = (P(("row", "col"), None), P("row", "col"), P("row", "col"))
    out_specs = P(("row", "col"), None)
    return jax.shard_map(local, mesh=mesh, in_specs=in_specs, out_specs=out_specs, check_vma=False)
```

time: 612 us -> 91.5 us (0.15)
  waiting for transfers between devices: 399 us -> 0 us
  blocking collectives: 189 us -> 0 us
  Pallas kernels: 0 us -> 86.6 us
  between operations: 13.4 us -> 0.01 us
  matrix products: 6.34 us -> 0 us
    psum x1 -> x0, waiting for transfers between devices: 296 us -> none  [broadcast(): return lax.psum(kept, axis)]
    psum x1 -> x0, blocking collectives: 165 us -> none  [local(): summed = lax.psum(partial_sum, 'row')]
    reduce_scatter x1 -> x0, waiting for transfers between devices: 103 us -> none  [local(): lax.psum_scatter(terms.astype(jnp.bfloat16), 'col', scatter_dimension=0,...]
    pallas_call x0 -> x1, Pallas kernels: none -> 86.6 us  [local(): pl.pallas_call(kernel, out_shape=jax.ShapeDtypeStruct((out, k), BF16), in...]
    all_gather x1 -> x0, blocking collectives: 24.5 us -> none  [local(): near = lax.all_gather(orbitals, 'col', axis=0, tiled=True)]
    dot_general x2 -> x0, matrix products: 6.34 us -> none  [the longest x1 4.42 us: local(): lax.dot_general(weighted, near, (((0,), (0,)), ((), ())), preferred_eleme...]
  transfers between devices with their start and end apart: 2 -> 0, of which waited for: 2 -> 0; matrix products, arithmetic and copies ran while one was open for 0% -> 0% of each run, Pallas kernels for 0% -> 0%
where the time goes in v1:
time: 91.5 us; the launch traced here: 91.2 us
  Pallas kernels  86.6 us (95%)
  local copies, waits for them, and re-layouts  4.6 us (5%)
    pallas_call x1, Pallas kernels, local(): pl.pallas_call(kernel, out_shape=jax.ShapeDtypeStruct((out, k), BF16), in...  86.6 us
    unnamed x7, local copies, waits for them, and re-layouts  4.6 us

profile of v1, /device:TPU:1, one launch (start us, length us, event | category | flops | bytes accessed | tf_op | source)
XLA Modules:
  0.0 91.2 jit_solution(4705368019530707109)
XLA Ops:
  0.0 0.0 copy-start
  0.0 1.9 %copy-done = f32[640,1280]{1,0:T(8,128)S(1)} copy-done((f32[640,1280]{1,0:T(8,128)S(1)}, f32[640,1280]{1,0:T(8,128)}, u32[]{:S(2)}) %copy-start) | copy-done | bytes 3276824
  1.9 0.0 copy-start.1
  1.9 1.3 %copy-done.1 = bf16[512,1280]{1,0:T(8,128)(2,1)S(1)} copy-done((bf16[512,1280]{1,0:T(8,128)(2,1)S(1)}, bf16[512,1280]{1,0:T(8,128)(2,1)}, u32[]{:S(2)}) %copy-start.1) | copy-done | bytes 1310744
  3.2 0.0 copy-start.2
  3.2 0.8 copy-done.2
  4.0 86.6 %shard_map.37 = bf16[32,384]{1,0:T(8,128)(2,1)S(1)} custom-call(bf16[40,384]{1,0:T(8,128)(2,1)S(1)} %copy-done.2, f32[640,1280]{1,0:T(8,128)S(1)} %copy-done, bf16[512,1280]{1,0:T(8,128)(2,1)S(1)} %copy-done.1), custom_call_target="tpu_custom_call" | custom-call | flops 1761607680 | bytes 4587520 | tf_op jit(solution)/shard_map/pallas_call | solution.py:239
  90.6 0.6 copy.5
Async XLA Ops:
  0.0 1.9 %copy-start = (f32[640,1280]{1,0:T(8,128)S(1)}, f32[640,1280]{1,0:T(8,128)}, u32[]{:S(2)}) copy-start(f32[640,1280]{1,0:T(8,128)} %coul_hbm.1) | copy-start | bytes 9830404
  1.9 1.3 %copy-start.1 = (bf16[512,1280]{1,0:T(8,128)(2,1)S(1)}, bf16[512,1280]{1,0:T(8,128)(2,1)}, u32[]{:S(2)}) copy-start(bf16[512,1280]{1,0:T(8,128)(2,1)} %interp_hbm.1) | copy-start | bytes 3932164
  3.2 0.8 copy-start.2

commit v2 on v1

v2 whole, which is shorter than its diff:
```python
import jax
import jax.numpy as jnp
from jax import lax
from jax.experimental import pallas as pl
from jax.experimental.pallas import tpu as pltpu
from jax.sharding import PartitionSpec as P

MESH = pl.DeviceIdType.MESH
Z, Y, L, X, C = 8, 4, 2, 4, 2
F32, BF16 = jnp.float32, jnp.bfloat16
H = 2


def device(z, y, l, x, core):
    return (z * Y + y, (l * X + x) * C + core)


def side_of(turn):
    return (2 + X - turn // C) % X


def core_of(turn):
    return (turn + turn // X) % C


def turn_of(side, core):
    half = (2 + X - side) % X
    return half * C + (core + half // 2) % C


def rows(slots):
    n, h, k = slots.shape
    return slots.astype(F32).reshape(n * h, k)


def kernel(
    orb, coul_hbm, interp_hbm, out,
    coul, coul_t, interp, near_s, near, far, acc_in, acc_out, part,
    y_out, y_in, con, con_f, con_m, relay, terms, pair_out, pair_in, fin_out, fin_in,
    local_sem, relay_sem, near_ss, near_rs, sib_ss, sib_rs, perm_ss, perm_rs,
    far_ss, far_rs, acc_ss, acc_rs, ys_ss, ys_rs, yg_ss, yg_rs,
    con_ss, con_rs, pair_sem, fin_ss, fin_rs,
):
    row, col = lax.axis_index("row"), lax.axis_index("col")
    z, y = row // Y, row % Y
    l, x, core = col // (X * C), (col // C) % X, col % C
    up, down = device((z + 1) % Z, y, l, x, core), device((z + Z - 1) % Z, y, l, x, core)
    up2, down2 = device((z + 2) % Z, y, l, x, core), device((z + Z - 2) % Z, y, l, x, core)
    sibling = device(z, y, l, x, 1 - core)
    chips = [None] + [((l + k // X) % L, (x + k % X) % X) for k in range(1, L * X)]
    came = [None] + [((l + k // X) % L, (x + X - k % X) % X) for k in range(1, L * X)]
    ahead = [None] + [(y + k) % Y for k in range(1, Y)]
    behind = [None] + [(y + Y - k) % Y for k in range(1, Y)]
    sends = []

    def send(src, dst, ss, rs, to):
        copy = pltpu.make_async_remote_copy(
            src_ref=src, dst_ref=dst, send_sem=ss, recv_sem=rs, device_id=to, device_id_type=MESH
        )
        copy.start()
        sends.append(copy)
        return copy

    load_coul = pltpu.make_async_copy(coul_hbm, coul, local_sem.at[0])
    load_interp = pltpu.make_async_copy(interp_hbm, interp, local_sem.at[1])
    load_coul.start()
    load_interp.start()

    home = (z + Z - col // C) % Z
    turn = turn_of((x + X - z % X) % X, core)
    first_to = device((z + turn) % Z, y, l, z % X, core)
    relayed = (z + Z - x) % Z
    other = jnp.where(core_of(relayed) == core, 0, 1)
    relayed = (relayed + other * X) % Z
    first_from = device(x + other * X, y, l, (x + side_of(relayed)) % X, core)
    piece = relayed * Y + (y % 2) * L + l
    targets = [device(z, j, other, x, y // 2) for j in range(Y)]
    own_target = (other == l) & (y // 2 == core)
    target_self = [own_target & (y == j) for j in range(Y)]
    sources = [device(z, core * 2 + j // L, j % L, x, core_of(home)) for j in range(Y)]
    source_self = [(s[0] == row) & (s[1] == col) for s in sources]

    barrier = pltpu.get_barrier_semaphore()
    greet = [first_from] + [device(z, y, *chips[k], core) for k in range(1, L * X)] + [sibling, up, down, up2, down2]
    greet += [device(z, ahead[k], l, x, core) for k in range(1, Y)]
    for j in range(Y):
        @pl.when(jnp.logical_not(source_self[j]))
        def _(j=j):
            pl.semaphore_signal(barrier, inc=1, device_id=sources[j], device_id_type=MESH)
    for d in greet:
        pl.semaphore_signal(barrier, inc=1, device_id=d, device_id_type=MESH)
    pl.semaphore_wait(barrier, jnp.where(own_target, len(greet) + Y - 1, len(greet) + Y))

    kind = piece % Y
    relay_c = send(orb, relay, relay_sem.at[0], relay_sem.at[1], first_to)

    def perm(j):
        return pltpu.make_async_remote_copy(
            src_ref=relay, dst_ref=far.at[piece], send_sem=perm_ss.at[j], recv_sem=perm_rs.at[kind],
            device_id=targets[j], device_id_type=MESH,
        )

    def finish():
        for c in sends:
            c.wait_send()
        for j in range(Y):
            @pl.when(jnp.logical_not(target_self[j]))
            def _(j=j):
                perm(j).wait_send()

    near_s[col] = orb[...]
    sib = [send(orb, near_s.at[col], sib_ss.at[0], sib_rs.at[0], sibling)]
    near_c = [None]
    for k in range(1, L * X):
        near_c.append(send(orb, near_s.at[col], near_ss.at[k], near_rs.at[k], device(z, y, *chips[k], core)))

    relay_c.wait_recv()
    for j in range(Y):
        @pl.when(jnp.logical_not(target_self[j]))
        def _(j=j):
            perm(j).start()

        @pl.when(target_self[j])
        def _():
            far[piece] = relay[...]

    load_coul.wait()
    for k in range(coul.shape[1] // 128):
        coul_t[pl.ds(128 * k, 128), :] = coul[:, pl.ds(128 * k, 128)].T

    parts = range(H)
    span = Y // H
    held = (range(H // 2), range(H // 2, H))

    def far_send(way, step, block, h):
        at = pl.ds(block * Y + h * span, span)
        return send(far.at[at], far.at[at], far_ss.at[way, step, h], far_rs.at[way, step, h], (up, down)[way])

    def acc_send(way, step, h):
        at = pl.ds(h * span, span)
        return send(
            acc_out.at[way, step, at], acc_in.at[way, step, at],
            acc_ss.at[way, step, h], acc_rs.at[way, step, h], (up, down)[way])

    def place(block, j):
        n = orb.shape[0]
        p = (j // L) * (L * X * C) + (j % L) * (X * C) + ((x + side_of(block)) % X) * C + core_of(block)
        return pl.ds(pl.multiple_of(p * n, n), n)

    def partial(block):
        points = rows(far[pl.ds(block * Y, Y)]).astype(BF16)
        density = lax.dot_general(points, near[...], (((1,), (1,)), ((), ())), preferred_element_type=F32)
        n = points.shape[0] // Y
        factor = jnp.concatenate([coul_t[place(block, j), :] for j in range(Y)], 0)
        weighted = (factor * density).astype(BF16)
        return jnp.dot(weighted, near[...], preferred_element_type=F32).reshape(Y, n, -1)

    far_c, acc_c = {}, {}
    for j in range(Y):
        @pl.when(jnp.logical_not(source_self[j]))
        def _(j=j):
            pltpu.make_async_remote_copy(
                src_ref=orb, dst_ref=far.at[home * Y + j], send_sem=perm_ss.at[j], recv_sem=perm_rs.at[j],
                device_id=sources[j], device_id_type=MESH,
            ).wait_recv()

        if (j + 1) % span == 0:
            for way in range(2):
                far_c[way, 0, j // span] = far_send(way, 0, home, j // span)
    for k in range(1, L * X):
        near_c[k].wait_recv()
        slot = (came[k][0] * X + came[k][1]) * C + core
        sib.append(send(near_s.at[slot], near_s.at[slot], sib_ss.at[k], sib_rs.at[k], sibling))

    for c in sib:
        c.wait_recv()
    near[...] = rows(near_s[...]).astype(BF16)

    own = partial(home)
    for way in range(2):
        for h in held[way]:
            at = slice(h * span, (h + 1) * span)
            acc_out[way, 0, at] = own[at].astype(BF16)
            acc_c[way, 0, h] = acc_send(way, 0, h)
    for step in range(1, 4):
        blocks = ((home + Z - step) % Z, (home + step) % Z)
        for h in parts:
            for way in range(2):
                far_c[way, step - 1, h].wait_recv()
                if step < 3 or h in held[way]:
                    far_c[way, step, h] = far_send(way, step, blocks[way], h)
        shares = [partial(blocks[way]) for way in range(2)]
        for h in parts:
            at = slice(h * span, (h + 1) * span)
            for way in range(2):
                share = shares[way][at]
                if (way, step - 1, h) in acc_c:
                    acc_c[way, step - 1, h].wait_recv()
                    share = share + acc_in[way, step - 1, at].astype(F32)
                acc_out[way, step, at] = share.astype(BF16)
                acc_c[way, step, h] = acc_send(way, step, h)
    for way in range(2):
        for h in held[way]:
            far_c[way, 3, h].wait_recv()
    block = (home + Z // 2) % Z
    share = partial(block)
    for h in parts:
        at = slice(h * span, (h + 1) * span)
        for way in range(2):
            acc_c[way, 3, h].wait_recv()
        total = share[at] + acc_in[0, 3, at].astype(F32) + acc_in[1, 3, at].astype(F32)
        part[at] = total
        y_out[at] = total.astype(BF16)

    ys = [None]
    for k in range(1, Y):
        ys.append(send(y_out.at[ahead[k]], y_in.at[k], ys_ss.at[k], ys_rs.at[k], device(z, ahead[k], l, x, core)))
    total = part[y]
    for k in range(1, Y):
        ys[k].wait_recv()
        total = total + y_in[k].astype(F32)
    mine = block * Y + y
    con[mine] = total.astype(BF16)
    def con_send(way, step, back, k):
        slot = ((block + (Z - back, back)[way]) % Z) * Y + spot[k]
        to = ((up, up2, up, up2), (down, down2, down, down2))[way][step]
        return send(con.at[slot], con.at[slot], con_ss.at[way, step, k], con_rs.at[way, step, k], to)

    spot = [y] + behind[1:]
    yg, con_c = {}, {}
    for k in (2, 1, 3):
        yg[k] = send(con.at[mine], con.at[mine], yg_ss.at[k], yg_rs.at[k], device(z, ahead[k], l, x, core))

    def begin(k):
        if k > 0:
            yg[k].wait_recv()
        for step in (1, 0):
            for way in range(2):
                con_c[way, step, k] = con_send(way, step, 0, k)

    def forward(k):
        for way in range(2):
            con_c[way, 1, k].wait_recv()
            if (k < 2) == (way == 0):
                con_c[way, 3, k] = con_send(way, 3, 2, k)
            con_c[way, 2, k] = con_send(way, 2, 2, k)

    def settle(b):
        for j in range(Y):
            con_f[place(b, j), :] = con[b * Y + j].astype(F32)

    begin(0)
    begin(1)
    begin(3)
    forward(0)
    begin(2)
    settle(block)
    for k in (1, 3, 2):
        forward(k)
    for way in range(2):
        for k in range(Y):
            con_c[way, 0, k].wait_recv()
        settle((block + (Z - 1, 1)[way]) % Z)
        settle((block + (Z - 2, 2)[way]) % Z)
    for way in range(2):
        for k in range(Y):
            con_c[way, 2, k].wait_recv()
        settle((block + (Z - 3, 3)[way]) % Z)
    load_interp.wait()
    for k in range(Y):
        con_c[0 if k < 2 else 1, 3, k].wait_recv()
    settle((block + 4) % Z)
    con_m[...] = con_f[...].astype(BF16)

    def term(half):
        tile = interp[:, half]
        return jnp.dot(tile.reshape(-1, tile.shape[-1]), con_m[...], preferred_element_type=F32).reshape(terms.shape)

    pair_out[...] = term(1 - core).astype(BF16)
    pair = send(pair_out, pair_in, pair_sem.at[0], pair_sem.at[1], sibling)
    both = term(core)
    pair.wait_recv()
    both = both + pair_in[...].astype(F32)
    terms[...] = both
    fin_out[...] = both.astype(BF16)
    fin = [None]
    for k in range(1, L * X):
        fin.append(send(
            fin_out.at[chips[k][0] * X + chips[k][1]], fin_in.at[k],
            fin_ss.at[k], fin_rs.at[k], device(z, y, *chips[k], core)))
    total = terms[l * X + x]
    for k in range(1, L * X):
        fin[k].wait_recv()
        total = total + fin_in[k].astype(F32)
    out[...] = total.astype(BF16)

    finish()


def local(orbitals, coulomb, interp):
    h, k = orbitals.shape
    m, n = coulomb.shape
    g = interp.shape[0]
    out = g // (L * X * C)
    dma = pltpu.SemaphoreType.DMA
    return pl.pallas_call(
        kernel,
        out_shape=jax.ShapeDtypeStruct((out, k), BF16),
        in_specs=[
            pl.BlockSpec(memory_space=pltpu.VMEM),
            pl.BlockSpec(memory_space=pltpu.HBM),
            pl.BlockSpec(memory_space=pltpu.HBM),
        ],
        out_specs=pl.BlockSpec(memory_space=pltpu.VMEM),
        scratch_shapes=[
            pltpu.VMEM((m, n), F32),
            pltpu.VMEM((n, m), F32),
            pltpu.VMEM((L * X, C, out, n), BF16),
            pltpu.VMEM((L * X * C, h, k), BF16),
            pltpu.VMEM((m, k), BF16),
            pltpu.VMEM((Z * Y, h, k), BF16),
            pltpu.VMEM((2, 4, Y, h, k), BF16),
            pltpu.VMEM((2, 4, Y, h, k), BF16),
            pltpu.VMEM((Y, h, k), F32),
            pltpu.VMEM((Y, h, k), BF16),
            pltpu.VMEM((Y, h, k), BF16),
            pltpu.VMEM((Z * Y, h, k), BF16),
            pltpu.VMEM((n, k), F32),
            pltpu.VMEM((n, k), BF16),
            pltpu.VMEM((h, k), BF16),
            pltpu.VMEM((L * X, out, k), F32),
            pltpu.VMEM((L * X, out, k), BF16),
            pltpu.VMEM((L * X, out, k), BF16),
            pltpu.VMEM((L * X, out, k), BF16),
            pltpu.VMEM((L * X, out, k), BF16),
            dma((2,)), dma((2,)), dma((8,)), dma((8,)), dma((8,)), dma((8,)), dma((4,)), dma((4,)),
            dma((2, 4, H)), dma((2, 4, H)), dma((2, 4, H)), dma((2, 4, H)), dma((4,)), dma((4,)), dma((4,)), dma((4,)),
            dma((2, 4, Y)), dma((2, 4, Y)), dma((2,)), dma((8,)), dma((8,)),
        ],
        compiler_params=pltpu.CompilerParams(
            collective_id=0, has_side_effects=True, vmem_limit_bytes=62 * 1024 * 1024
        ),
        cost_estimate=pl.CostEstimate(
            flops=4 * m * n * k + 2 * g * n * k, bytes_accessed=4 * m * n + 2 * g * n, transcendentals=0
        ),
    )(orbitals, coulomb, interp.reshape(L * X, C, out, n))


def solution(mesh):
    in_specs = (P(("row", "col"), None), P("row", "col"), P("row", "col"))
    out_specs = P(("row", "col"), None)
    return jax.shard_map(local, mesh=mesh, in_specs=in_specs, out_specs=out_specs, check_vma=False)
```

time: 91.5 us -> 79.8 us (0.87)
  Pallas kernels: 86.6 us -> 78.2 us
  local copies, waits for them, and re-layouts: 4.6 us -> 1.35 us
    pallas_call x1, Pallas kernels: 86.6 us -> 78.2 us  [local(): pl.pallas_call(kernel, out_shape=jax.ShapeDtypeStruct((out, k), BF16), in...]
    unnamed x7 -> x1, local copies, waits for them, and re-layouts: 4.6 us -> 1.35 us
where the time goes in v2:
time: 79.8 us; the launch traced here: 79.5 us
  Pallas kernels  78.2 us (98%)
  local copies, waits for them, and re-layouts  1.35 us (2%)
    pallas_call x1, Pallas kernels, local(): pl.pallas_call(kernel, out_shape=jax.ShapeDtypeStruct((out, k), BF16), in...  78.2 us

profile of v2, /device:TPU:1, one launch (start us, length us, event | category | flops | bytes accessed | tf_op | source)
XLA Modules:
  0.0 79.5 jit_solution(10161601966359003596)
XLA Ops:
  0.0 78.2 %shard_map.37 = bf16[32,384]{1,0:T(8,128)(2,1)} custom-call(bf16[40,384]{1,0:T(8,128)(2,1)} %orb.1, f32[640,1280]{1,0:T(8,128)} %coul_hbm.1, bf16[8,2,32,1280]{3,2,1,0:T(8,128)(2,1)} %bitcast.1), custom_call_target="tpu_custom_call" | custom-call | flops 1761607680 | bytes 4587520 | tf_op jit(solution)/shard_map/pallas_call | solution.py:306
  78.2 1.3 %copy.5 = bf16[32,384]{1,0:T(8,128)(2,1)} copy(bf16[32,384]{1,0:T(8,128)(2,1)} %shard_map.37) | data formatting | bytes 49152

commit v3 on v2

--- a/solution.py
+++ b/solution.py
@@ -8,7 +8,7 @@
 MESH = pl.DeviceIdType.MESH
 Z, Y, L, X, C = 8, 4, 2, 4, 2
 F32, BF16 = jnp.float32, jnp.bfloat16
-H = 2
+H = 4
 
 
 def device(z, y, l, x, core):
@@ -38,14 +38,14 @@
     coul, coul_t, interp, near_s, near, far, acc_in, acc_out, part,
     y_out, y_in, con, con_f, con_m, relay, terms, pair_out, pair_in, fin_out, fin_in,
     local_sem, relay_sem, near_ss, near_rs, sib_ss, sib_rs, perm_ss, perm_rs,
-    far_ss, far_rs, acc_ss, acc_rs, ys_ss, ys_rs, yg_ss, yg_rs,
-    con_ss, con_rs, pair_sem, fin_ss, fin_rs,
+    far_ss, far_rs, acc_ss, acc_rs, ys_ss, ys_rs,
+    con_ss, con_rs, pair_ss, pair_rs, fin_ss, fin_rs,
 ):
     row, col = lax.axis_index("row"), lax.axis_index("col")
     z, y = row // Y, row % Y
     l, x, core = col // (X * C), (col // C) % X, col % C
     up, down = device((z + 1) % Z, y, l, x, core), device((z + Z - 1) % Z, y, l, x, core)
-    up2, down2 = device((z + 2) % Z, y, l, x, core), device((z + Z - 2) % Z, y, l, x, core)
+    plane = [device((z + d) % Z, y, l, x, core) for d in range(Z)]
     sibling = device(z, y, l, x, 1 - core)
     chips = [None] + [((l + k // X) % L, (x + k % X) % X) for k in range(1, L * X)]
     came = [None] + [((l + k // X) % L, (x + X - k % X) % X) for k in range(1, L * X)]
@@ -81,7 +81,7 @@
     source_self = [(s[0] == row) & (s[1] == col) for s in sources]
 
     barrier = pltpu.get_barrier_semaphore()
-    greet = [first_from] + [device(z, y, *chips[k], core) for k in range(1, L * X)] + [sibling, up, down, up2, down2]
+    greet = [first_from] + [device(z, y, *chips[k], core) for k in range(1, L * X)] + [sibling] + plane[1:]
     greet += [device(z, ahead[k], l, x, core) for k in range(1, Y)]
     for j in range(Y):
         @pl.when(jnp.logical_not(source_self[j]))
@@ -103,6 +103,10 @@
     def finish():
         for c in sends:
             c.wait_send()
+        for j in range(Y):
+            @pl.when(y != j)
+            def _(j=j):
+                y_send(j).wait_send()
         for j in range(Y):
             @pl.when(jnp.logical_not(target_self[j]))
             def _(j=j):
@@ -202,6 +206,13 @@
     for way in range(2):
         for h in held[way]:
             far_c[way, 3, h].wait_recv()
+    def y_send(j):
+        k = (j + Y - y) % Y
+        return pltpu.make_async_remote_copy(
+            src_ref=y_out.at[j], dst_ref=y_in.at[k], send_sem=ys_ss.at[k], recv_sem=ys_rs.at[k],
+            device_id=device(z, j, l, x, core), device_id_type=MESH,
+        )
+
     block = (home + Z // 2) % Z
     share = partial(block)
     for h in parts:
@@ -211,87 +222,90 @@
         total = share[at] + acc_in[0, 3, at].astype(F32) + acc_in[1, 3, at].astype(F32)
         part[at] = total
         y_out[at] = total.astype(BF16)
-
-    ys = [None]
-    for k in range(1, Y):
-        ys.append(send(y_out.at[ahead[k]], y_in.at[k], ys_ss.at[k], ys_rs.at[k], device(z, ahead[k], l, x, core)))
+        for j in range(h * span, (h + 1) * span):
+            @pl.when(y != j)
+            def _(j=j):
+                y_send(j).start()
+
     total = part[y]
     for k in range(1, Y):
-        ys[k].wait_recv()
+        pltpu.make_async_remote_copy(
+            src_ref=y_out.at[0], dst_ref=y_in.at[k], send_sem=ys_ss.at[k], recv_sem=ys_rs.at[k],
+            device_id=device(z, behind[k], l, x, core), device_id_type=MESH,
+        ).wait_recv()
         total = total + y_in[k].astype(F32)
     mine = block * Y + y
     con[mine] = total.astype(BF16)
-    def con_send(way, step, back, k):
-        slot = ((block + (Z - back, back)[way]) % Z) * Y + spot[k]
-        to = ((up, up2, up, up2), (down, down2, down, down2))[way][step]
-        return send(con.at[slot], con.at[slot], con_ss.at[way, step, k], con_rs.at[way, step, k], to)
-
-    spot = [y] + behind[1:]
-    yg, con_c = {}, {}
+    def con_send(d, k):
+        if d in (3, 4, 5):
+            slot, to = (block + Z - d) % Z * Y + y, device(z, ahead[k], l, x, core)
+        else:
+            slot, to = block * Y + behind[k], plane[d]
+        return send(con.at[slot], con.at[slot], con_ss.at[d, k], con_rs.at[d, k], to)
+
+    def con_wait(d, k):
+        con_c[d, k].wait_recv()
+        settle((block + Z - d) % Z, behind[k] if k > 0 else y)
+
+    def settle(b, j):
+        con_f[place(b, j), :] = con[b * Y + j].astype(F32)
+
+    con_c = {}
     for k in (2, 1, 3):
-        yg[k] = send(con.at[mine], con.at[mine], yg_ss.at[k], yg_rs.at[k], device(z, ahead[k], l, x, core))
-
-    def begin(k):
-        if k > 0:
-            yg[k].wait_recv()
-        for step in (1, 0):
-            for way in range(2):
-                con_c[way, step, k] = con_send(way, step, 0, k)
-
-    def forward(k):
-        for way in range(2):
-            con_c[way, 1, k].wait_recv()
-            if (k < 2) == (way == 0):
-                con_c[way, 3, k] = con_send(way, 3, 2, k)
-            con_c[way, 2, k] = con_send(way, 2, 2, k)
-
-    def settle(b):
-        for j in range(Y):
-            con_f[place(b, j), :] = con[b * Y + j].astype(F32)
-
-    begin(0)
-    begin(1)
-    begin(3)
-    forward(0)
-    begin(2)
-    settle(block)
+        con_c[0, k] = send(
+            con.at[mine], con.at[mine], con_ss.at[0, k], con_rs.at[0, k], device(z, ahead[k], l, x, core))
+    for d in (4, 3, 5, 2, 6, 1, 7):
+        con_c[d, 0] = send(
+            con.at[mine], con.at[mine], con_ss.at[d, 0], con_rs.at[d, 0], plane[d])
+    settle(block, y)
+    for step in ((0, 1), (0, 3), (3, 0), (5, 0), (0, 2), (4, 0)):
+        d, k = step
+        con_c[d, k].wait_recv()
+        if d == 0:
+            for e in (2, 6, 1, 7):
+                con_c[e, k] = con_send(e, k)
+        else:
+            for e in (2, 1, 3):
+                con_c[d, e] = con_send(d, e)
+        settle((block + Z - d) % Z, behind[k] if k > 0 else y)
+    for d in (1, 7, 2, 6):
+        con_wait(d, 0)
     for k in (1, 3, 2):
-        forward(k)
-    for way in range(2):
-        for k in range(Y):
-            con_c[way, 0, k].wait_recv()
-        settle((block + (Z - 1, 1)[way]) % Z)
-        settle((block + (Z - 2, 2)[way]) % Z)
-    for way in range(2):
-        for k in range(Y):
-            con_c[way, 2, k].wait_recv()
-        settle((block + (Z - 3, 3)[way]) % Z)
+        for d in (1, 7, 2, 6):
+            con_wait(d, k)
+    for d in (3, 5, 4):
+        for k in (1, 3, 2):
+            con_wait(d, k)
     load_interp.wait()
-    for k in range(Y):
-        con_c[0 if k < 2 else 1, 3, k].wait_recv()
-    settle((block + 4) % Z)
     con_m[...] = con_f[...].astype(BF16)
 
-    def term(half):
-        tile = interp[:, half]
-        return jnp.dot(tile.reshape(-1, tile.shape[-1]), con_m[...], preferred_element_type=F32).reshape(terms.shape)
-
-    pair_out[...] = term(1 - core).astype(BF16)
-    pair = send(pair_out, pair_in, pair_sem.at[0], pair_sem.at[1], sibling)
-    both = term(core)
-    pair.wait_recv()
-    both = both + pair_in[...].astype(F32)
-    terms[...] = both
-    fin_out[...] = both.astype(BF16)
-    fin = [None]
-    for k in range(1, L * X):
-        fin.append(send(
-            fin_out.at[chips[k][0] * X + chips[k][1]], fin_in.at[k],
-            fin_ss.at[k], fin_rs.at[k], device(z, y, *chips[k], core)))
-    total = terms[l * X + x]
-    for k in range(1, L * X):
-        fin[k].wait_recv()
-        total = total + fin_in[k].astype(F32)
+    def term(to, half):
+        tile = interp[pl.ds(to * X, X), half]
+        return jnp.dot(
+            tile.reshape(-1, tile.shape[-1]), con_m[...], preferred_element_type=F32).reshape(X, *terms.shape[1:])
+
+    order = ((1, 1 - l), (0, l))
+    pair = {}
+    for i, to in order:
+        pair_out[i] = term(to, 1 - core).astype(BF16)
+        pair[i] = send(pair_out.at[i], pair_in.at[i], pair_ss.at[i], pair_rs.at[i], sibling)
+    fin = {}
+    for i, to in order:
+        both = term(to, core)
+        pair[i].wait_recv()
+        both = both + pair_in[i].astype(F32)
+        fin_out[i] = both.astype(BF16)
+        if i == 0:
+            terms[...] = both
+        for k in (2, 1, 3, 0):
+            if (i, k) != (0, 0):
+                fin[i, k] = send(
+                    fin_out.at[i, (x + k) % X], fin_in.at[i, k], fin_ss.at[i * X + k], fin_rs.at[i * X + k],
+                    device(z, y, (l + i) % L, (x + k) % X, core))
+    total = terms[x]
+    for i, k in fin:
+        fin[i, k].wait_recv()
+        total = total + fin_in[i, k].astype(F32)
     out[...] = total.astype(BF16)
 
     finish()
@@ -328,14 +342,14 @@
             pltpu.VMEM((n, k), F32),
             pltpu.VMEM((n, k), BF16),
             pltpu.VMEM((h, k), BF16),
-            pltpu.VMEM((L * X, out, k), F32),
-            pltpu.VMEM((L * X, out, k), BF16),
-            pltpu.VMEM((L * X, out, k), BF16),
-            pltpu.VMEM((L * X, out, k), BF16),
-            pltpu.VMEM((L * X, out, k), BF16),
+            pltpu.VMEM((X, out, k), F32),
+            pltpu.VMEM((L, X, out, k), BF16),
+            pltpu.VMEM((L, X, out, k), BF16),
+            pltpu.VMEM((L, X, out, k), BF16),
+            pltpu.VMEM((L, X, out, k), BF16),
             dma((2,)), dma((2,)), dma((8,)), dma((8,)), dma((8,)), dma((8,)), dma((4,)), dma((4,)),
-            dma((2, 4, H)), dma((2, 4, H)), dma((2, 4, H)), dma((2, 4, H)), dma((4,)), dma((4,)), dma((4,)), dma((4,)),
-            dma((2, 4, Y)), dma((2, 4, Y)), dma((2,)), dma((8,)), dma((8,)),
+            dma((2, 4, H)), dma((2, 4, H)), dma((2, 4, H)), dma((2, 4, H)), dma((4,)), dma((4,)),
+            dma((Z, Y)), dma((Z, Y)), dma((2,)), dma((2,)), dma((8,)), dma((8,)),
         ],
         compiler_params=pltpu.CompilerParams(
             collective_id=0, has_side_effects=True, vmem_limit_bytes=62 * 1024 * 1024

time: 79.8 us -> 75.5 us (0.946)
  Pallas kernels: 78.2 us -> 74 us
    pallas_call x1, Pallas kernels: 78.2 us -> 74 us  [local(): pl.pallas_call(kernel, out_shape=jax.ShapeDtypeStruct((out, k), BF16), in...]
where the time goes in v3:
time: 75.5 us; the launch traced here: 75.3 us
  Pallas kernels  74 us (98%)
  local copies, waits for them, and re-layouts  1.35 us (2%)
    pallas_call x1, Pallas kernels, local(): pl.pallas_call(kernel, out_shape=jax.ShapeDtypeStruct((out, k), BF16), in...  74 us

profile of v3, /device:TPU:1, one launch (start us, length us, event | category | flops | bytes accessed | tf_op | source)
XLA Modules:
  0.0 75.3 jit_solution(3162184955473681068)
XLA Ops:
  0.0 74.0 %shard_map.37 = bf16[32,384]{1,0:T(8,128)(2,1)} custom-call(bf16[40,384]{1,0:T(8,128)(2,1)} %orb.1, f32[640,1280]{1,0:T(8,128)} %coul_hbm.1, bf16[8,2,32,1280]{3,2,1,0:T(8,128)(2,1)} %bitcast.1), custom_call_target="tpu_custom_call" | custom-call | flops 1761607680 | bytes 4587520 | tf_op jit(solution)/shard_map/pallas_call | solution.py:320
  74.0 1.3 %copy.5 = bf16[32,384]{1,0:T(8,128)(2,1)} copy(bf16[32,384]{1,0:T(8,128)(2,1)} %shard_map.37) | data formatting | bytes 49152

commit v4 on v3

--- a/solution.py
+++ b/solution.py
@@ -15,17 +15,25 @@
     return (z * Y + y, (l * X + x) * C + core)
 
 
+def mod(a, n):
+    return a % n if isinstance(a, int) else lax.rem(a, n)
+
+
+def div(a, n):
+    return a // n if isinstance(a, int) else lax.div(a, n)
+
+
 def side_of(turn):
-    return (2 + X - turn // C) % X
+    return mod(2 + X - div(turn, C), X)
 
 
 def core_of(turn):
-    return (turn + turn // X) % C
+    return mod(turn + div(turn, X), C)
 
 
 def turn_of(side, core):
-    half = (2 + X - side) % X
-    return half * C + (core + half // 2) % C
+    half = mod(2 + X - side, X)
+    return half * C + mod(core + div(half, 2), C)
 
 
 def rows(slots):
@@ -42,15 +50,15 @@
     con_ss, con_rs, pair_ss, pair_rs, fin_ss, fin_rs,
 ):
     row, col = lax.axis_index("row"), lax.axis_index("col")
-    z, y = row // Y, row % Y
-    l, x, core = col // (X * C), (col // C) % X, col % C
-    up, down = device((z + 1) % Z, y, l, x, core), device((z + Z - 1) % Z, y, l, x, core)
-    plane = [device((z + d) % Z, y, l, x, core) for d in range(Z)]
+    z, y = div(row, Y), mod(row, Y)
+    l, x, core = div(col, X * C), mod(div(col, C), X), mod(col, C)
+    up, down = device(mod(z + 1, Z), y, l, x, core), device(mod(z + Z - 1, Z), y, l, x, core)
+    plane = [device(mod(z + d, Z), y, l, x, core) for d in range(Z)]
     sibling = device(z, y, l, x, 1 - core)
-    chips = [None] + [((l + k // X) % L, (x + k % X) % X) for k in range(1, L * X)]
-    came = [None] + [((l + k // X) % L, (x + X - k % X) % X) for k in range(1, L * X)]
-    ahead = [None] + [(y + k) % Y for k in range(1, Y)]
-    behind = [None] + [(y + Y - k) % Y for k in range(1, Y)]
+    chips = [None] + [(mod(l + k // X, L), mod(x + mod(k, X), X)) for k in range(1, L * X)]
+    came = [None] + [(mod(l + k // X, L), mod(x + X - mod(k, X), X)) for k in range(1, L * X)]
+    ahead = [None] + [mod(y + k, Y) for k in range(1, Y)]
+    behind = [None] + [mod(y + Y - k, Y) for k in range(1, Y)]
     sends = []
 
     def send(src, dst, ss, rs, to):
@@ -61,37 +69,36 @@
         sends.append(copy)
         return copy
 
+    home = mod(z + Z - div(col, C), Z)
+    turn = turn_of(mod(x + X - mod(z, X), X), core)
+    first_to = device(mod(z + turn, Z), y, l, mod(z, X), core)
+    relayed = mod(z + Z - x, Z)
+    other = jnp.where(core_of(relayed) == core, 0, 1)
+    relayed = mod(relayed + other * X, Z)
+    first_from = device(x + other * X, y, l, mod(x + side_of(relayed), X), core)
+    piece = relayed * Y + (y % 2) * L + l
+    targets = [device(z, mod(y + k, Y), other, x, div(y, 2)) for k in range(Y)]
+    own_target = (other == l) & (div(y, 2) == core)
+    sources = [device(z, core * 2 + j // L, mod(j, L), x, core_of(home)) for j in range(Y)]
+    source_self = [(s[0] == row) & (s[1] == col) for s in sources]
+
+    barrier = pltpu.get_barrier_semaphore()
+    greet = [first_from] + [device(z, y, *chips[k], core) for k in range(1, L * X)] + [sibling] + plane[1:]
+    greet += [device(z, ahead[k], l, x, core) for k in range(1, Y)]
+    for d in greet:
+        pl.semaphore_signal(barrier, inc=1, device_id=d, device_id_type=MESH)
+    for j in range(Y):
+        @pl.when(jnp.logical_not(source_self[j]))
+        def _(j=j):
+            pl.semaphore_signal(barrier, inc=1, device_id=sources[j], device_id_type=MESH)
     load_coul = pltpu.make_async_copy(coul_hbm, coul, local_sem.at[0])
     load_interp = pltpu.make_async_copy(interp_hbm, interp, local_sem.at[1])
     load_coul.start()
     load_interp.start()
 
-    home = (z + Z - col // C) % Z
-    turn = turn_of((x + X - z % X) % X, core)
-    first_to = device((z + turn) % Z, y, l, z % X, core)
-    relayed = (z + Z - x) % Z
-    other = jnp.where(core_of(relayed) == core, 0, 1)
-    relayed = (relayed + other * X) % Z
-    first_from = device(x + other * X, y, l, (x + side_of(relayed)) % X, core)
-    piece = relayed * Y + (y % 2) * L + l
-    targets = [device(z, j, other, x, y // 2) for j in range(Y)]
-    own_target = (other == l) & (y // 2 == core)
-    target_self = [own_target & (y == j) for j in range(Y)]
-    sources = [device(z, core * 2 + j // L, j % L, x, core_of(home)) for j in range(Y)]
-    source_self = [(s[0] == row) & (s[1] == col) for s in sources]
-
-    barrier = pltpu.get_barrier_semaphore()
-    greet = [first_from] + [device(z, y, *chips[k], core) for k in range(1, L * X)] + [sibling] + plane[1:]
-    greet += [device(z, ahead[k], l, x, core) for k in range(1, Y)]
-    for j in range(Y):
-        @pl.when(jnp.logical_not(source_self[j]))
-        def _(j=j):
-            pl.semaphore_signal(barrier, inc=1, device_id=sources[j], device_id_type=MESH)
-    for d in greet:
-        pl.semaphore_signal(barrier, inc=1, device_id=d, device_id_type=MESH)
     pl.semaphore_wait(barrier, jnp.where(own_target, len(greet) + Y - 1, len(greet) + Y))
 
-    kind = piece % Y
+    kind = mod(piece, Y)
     relay_c = send(orb, relay, relay_sem.at[0], relay_sem.at[1], first_to)
 
     def perm(j):
@@ -107,10 +114,12 @@
             @pl.when(y != j)
             def _(j=j):
                 y_send(j).wait_send()
-        for j in range(Y):
-            @pl.when(jnp.logical_not(target_self[j]))
-            def _(j=j):
-                perm(j).wait_send()
+        for j in range(1, Y):
+            perm(j).wait_send()
+
+        @pl.when(jnp.logical_not(own_target))
+        def _():
+            perm(0).wait_send()
 
     near_s[col] = orb[...]
     sib = [send(orb, near_s.at[col], sib_ss.at[0], sib_rs.at[0], sibling)]
@@ -119,14 +128,16 @@
         near_c.append(send(orb, near_s.at[col], near_ss.at[k], near_rs.at[k], device(z, y, *chips[k], core)))
 
     relay_c.wait_recv()
-    for j in range(Y):
-        @pl.when(jnp.logical_not(target_self[j]))
-        def _(j=j):
-            perm(j).start()
-
-        @pl.when(target_self[j])
-        def _():
-            far[piece] = relay[...]
+    for j in (2, 1, 3):
+        perm(j).start()
+
+    @pl.when(jnp.logical_not(own_target))
+    def _():
+        perm(0).start()
+
+    @pl.when(own_target)
+    def _():
+        far[piece] = relay[...]
 
     load_coul.wait()
     for k in range(coul.shape[1] // 128):
@@ -148,7 +159,7 @@
 
     def place(block, j):
         n = orb.shape[0]
-        p = (j // L) * (L * X * C) + (j % L) * (X * C) + ((x + side_of(block)) % X) * C + core_of(block)
+        p = (j // L) * (L * X * C) + (mod(j, L)) * (X * C) + (mod(x + side_of(block), X)) * C + core_of(block)
         return pl.ds(pl.multiple_of(p * n, n), n)
 
     def partial(block):
@@ -187,7 +198,7 @@
             acc_out[way, 0, at] = own[at].astype(BF16)
             acc_c[way, 0, h] = acc_send(way, 0, h)
     for step in range(1, 4):
-        blocks = ((home + Z - step) % Z, (home + step) % Z)
+        blocks = (mod(home + Z - step, Z), mod(home + step, Z))
         for h in parts:
             for way in range(2):
                 far_c[way, step - 1, h].wait_recv()
@@ -207,13 +218,13 @@
         for h in held[way]:
             far_c[way, 3, h].wait_recv()
     def y_send(j):
-        k = (j + Y - y) % Y
+        k = mod(j + Y - y, Y)
         return pltpu.make_async_remote_copy(
             src_ref=y_out.at[j], dst_ref=y_in.at[k], send_sem=ys_ss.at[k], recv_sem=ys_rs.at[k],
             device_id=device(z, j, l, x, core), device_id_type=MESH,
         )
 
-    block = (home + Z // 2) % Z
+    block = mod(home + Z // 2, Z)
     share = partial(block)
     for h in parts:
         at = slice(h * span, (h + 1) * span)
@@ -238,14 +249,14 @@
     con[mine] = total.astype(BF16)
     def con_send(d, k):
         if d in (3, 4, 5):
-            slot, to = (block + Z - d) % Z * Y + y, device(z, ahead[k], l, x, core)
+            slot, to = mod(block + Z - d, Z) * Y + y, device(z, ahead[k], l, x, core)
         else:
             slot, to = block * Y + behind[k], plane[d]
         return send(con.at[slot], con.at[slot], con_ss.at[d, k], con_rs.at[d, k], to)
 
     def con_wait(d, k):
         con_c[d, k].wait_recv()
-        settle((block + Z - d) % Z, behind[k] if k > 0 else y)
+        settle(mod(block + Z - d, Z), behind[k] if k > 0 else y)
 
     def settle(b, j):
         con_f[place(b, j), :] = con[b * Y + j].astype(F32)
@@ -267,7 +278,7 @@
         else:
             for e in (2, 1, 3):
                 con_c[d, e] = con_send(d, e)
-        settle((block + Z - d) % Z, behind[k] if k > 0 else y)
+        settle(mod(block + Z - d, Z), behind[k] if k > 0 else y)
     for d in (1, 7, 2, 6):
         con_wait(d, 0)
     for k in (1, 3, 2):
@@ -300,8 +311,8 @@
         for k in (2, 1, 3, 0):
             if (i, k) != (0, 0):
                 fin[i, k] = send(
-                    fin_out.at[i, (x + k) % X], fin_in.at[i, k], fin_ss.at[i * X + k], fin_rs.at[i * X + k],
-                    device(z, y, (l + i) % L, (x + k) % X, core))
+                    fin_out.at[i, mod(x + k, X)], fin_in.at[i, k], fin_ss.at[i * X + k], fin_rs.at[i * X + k],
+                    device(z, y, mod(l + i, L), mod(x + k, X), core))
     total = terms[x]
     for i, k in fin:
         fin[i, k].wait_recv()

time: 75.5 us -> 75 us (level)
  no operation moved by 1% of the time
where the time goes in v4:
time: 75 us; the launch traced here: 74.7 us
  Pallas kernels  73.4 us (98%)
  local copies, waits for them, and re-layouts  1.35 us (2%)
    pallas_call x1, Pallas kernels, local(): pl.pallas_call(kernel, out_shape=jax.ShapeDtypeStruct((out, k), BF16), in...  73.4 us

profile of v4, /device:TPU:1, one launch (start us, length us, event | category | flops | bytes accessed | tf_op | source)
XLA Modules:
  0.0 74.7 jit_solution(10182276278349286472)
XLA Ops:
  0.0 73.4 %shard_map.37 = bf16[32,384]{1,0:T(8,128)(2,1)} custom-call(bf16[40,384]{1,0:T(8,128)(2,1)} %orb.1, f32[640,1280]{1,0:T(8,128)} %coul_hbm.1, bf16[8,2,32,1280]{3,2,1,0:T(8,128)(2,1)} %bitcast.1), custom_call_target="tpu_custom_call" | custom-call | flops 1761607680 | bytes 4587520 | tf_op jit(solution)/shard_map/pallas_call | solution.py:331
  73.4 1.3 %copy.5 = bf16[32,384]{1,0:T(8,128)(2,1)} copy(bf16[32,384]{1,0:T(8,128)(2,1)} %shard_map.37) | data formatting | bytes 49152

commit v5 on v4

--- a/solution.py
+++ b/solution.py
@@ -269,7 +269,7 @@
         con_c[d, 0] = send(
             con.at[mine], con.at[mine], con_ss.at[d, 0], con_rs.at[d, 0], plane[d])
     settle(block, y)
-    for step in ((0, 1), (0, 3), (3, 0), (5, 0), (0, 2), (4, 0)):
+    for step in ((0, 1), (0, 3), (3, 0), (5, 0), (4, 0), (0, 2)):
         d, k = step
         con_c[d, k].wait_recv()
         if d == 0:

time: 75 us -> 75 us (level)
  no operation moved by 1% of the time
where the time goes in v5:
time: 75 us; the launch traced here: 74.7 us
  Pallas kernels  73.4 us (98%)
  local copies, waits for them, and re-layouts  1.35 us (2%)
    pallas_call x1, Pallas kernels, local(): pl.pallas_call(kernel, out_shape=jax.ShapeDtypeStruct((out, k), BF16), in...  73.4 us

profile of v5, /device:TPU:1, one launch (start us, length us, event | category | flops | bytes accessed | tf_op | source)
XLA Modules:
  0.0 74.7 jit_solution(1844609890375656790)
XLA Ops:
  0.0 73.4 %shard_map.37 = bf16[32,384]{1,0:T(8,128)(2,1)} custom-call(bf16[40,384]{1,0:T(8,128)(2,1)} %orb.1, f32[640,1280]{1,0:T(8,128)} %coul_hbm.1, bf16[8,2,32,1280]{3,2,1,0:T(8,128)(2,1)} %bitcast.1), custom_call_target="tpu_custom_call" | custom-call | flops 1761607680 | bytes 4587520 | tf_op jit(solution)/shard_map/pallas_call | solution.py:331
  73.4 1.3 %copy.5 = bf16[32,384]{1,0:T(8,128)(2,1)} copy(bf16[32,384]{1,0:T(8,128)(2,1)} %shard_map.37) | data formatting | bytes 49152

commit v6 on v4

--- a/solution.py
+++ b/solution.py
@@ -8,7 +8,7 @@
 MESH = pl.DeviceIdType.MESH
 Z, Y, L, X, C = 8, 4, 2, 4, 2
 F32, BF16 = jnp.float32, jnp.bfloat16
-H = 4
+H = 2
 
 
 def device(z, y, l, x, core):

time: 75 us -> 74.6 us (level)
  no operation moved by 1% of the time
where the time goes in v6:
time: 74.6 us; the launch traced here: 74.4 us
  Pallas kernels  73 us (98%)
  local copies, waits for them, and re-layouts  1.35 us (2%)
    pallas_call x1, Pallas kernels, local(): pl.pallas_call(kernel, out_shape=jax.ShapeDtypeStruct((out, k), BF16), in...  73 us

profile of v6, /device:TPU:1, one launch (start us, length us, event | category | flops | bytes accessed | tf_op | source)
XLA Modules:
  0.0 74.4 jit_solution(18174145368685255439)
XLA Ops:
  0.0 73.0 %shard_map.37 = bf16[32,384]{1,0:T(8,128)(2,1)} custom-call(bf16[40,384]{1,0:T(8,128)(2,1)} %orb.1, f32[640,1280]{1,0:T(8,128)} %coul_hbm.1, bf16[8,2,32,1280]{3,2,1,0:T(8,128)(2,1)} %bitcast.1), custom_call_target="tpu_custom_call" | custom-call | flops 1761607680 | bytes 4587520 | tf_op jit(solution)/shard_map/pallas_call | solution.py:331
  73.0 1.3 %copy.5 = bf16[32,384]{1,0:T(8,128)(2,1)} copy(bf16[32,384]{1,0:T(8,128)(2,1)} %shard_map.37) | data formatting | bytes 49152
